TPU v7x, 32 devices: a whole 2x2x4 slice. The times are simulated.
32 devices in a mesh: ctx: 8 (over z, y), head: 4 (over x, core).
Axes of the slice: x: 2, y: 2, z: 4, core: 2. Of those that a mesh axis runs over, the one named last changes fastest.
Arguments:
- layer_input: bfloat16 [2048, 2048], P('ctx', 'head'), may hold values from -6 to 6
- queries: bfloat16 [2048, 1024], P('ctx', 'head'), may hold values from -6 to 6
- keys: bfloat16 [2048, 512], P('ctx', 'head'), may hold values from -6 to 6
- values: bfloat16 [2048, 512], P('ctx', 'head'), may hold values from -6 to 6
- result_cotangent: bfloat16 [2048, 1024], P('ctx', 'head'), may hold values from -0.3125 to 0.3125
- log_decay: float32 [4, 2048], P('head', 'ctx'), may hold values from -2 to 0
Outputs:
- weight_k_grad: bfloat16 [2048, 512], P('ctx', 'head')
- weight_v_grad: bfloat16 [2048, 512], P('ctx', 'head')
All inputs are finite; a program needn't handle non-finite values.
Results may differ from a plain program's by a relative error of at most 0.0057.
Values may be sent and summed in bfloat16 or wider, within the bound.
A program may use at most 64 MiB of HBM per device.

v0:
```python
import jax
import jax.numpy as jnp
from jax import lax
from jax.sharding import PartitionSpec as P

E = 128
WINDOW = 256


neg_fill = -1e30


def entering(array, axis, combine, identity):
    size, position = (lax.axis_size(axis), lax.axis_index(axis))
    everything = jax.tree.map(lambda part: lax.all_gather(part, axis), array)
    start = jax.tree.map(
        lambda part, zero: jnp.broadcast_to(jnp.asarray(zero, part.dtype), part.shape),
        array,
        identity,
    )

    def turn(k, before):
        at = size - 1 - k
        reached = at > position
        new = combine(before, jax.tree.map(lambda part: part[at], everything))
        return jax.tree.map(lambda a, b: jnp.where(reached, a, b), new, before)

    return lax.fori_loop(0, size, turn, start)


def shifted(value, axis, steps):
    count = lax.axis_size(axis)
    leading, last = (max(0, -steps), min(count, count - steps))
    return lax.ppermute(value, axis, [(source, source + steps) for source in range(leading, last)])


def band_grads(q_block, h_block, key_rows, value_rows, query_pos, key_pos):
    head_dim = key_rows.shape[1]
    group_size = q_block.shape[1] // head_dim
    row_count = q_block.shape[0]
    q_heads = q_block.reshape(row_count, group_size, head_dim)
    h_heads = h_block.reshape(row_count, group_size, head_dim)
    factor = head_dim ** (-0.5)
    scores = (
        jnp.einsum("trd,jd->rtj", q_heads, key_rows, preferred_element_type=jnp.float32) * factor
    )
    offset = query_pos[:, None] - key_pos[None, :]
    inside = (offset >= 0) & (offset < WINDOW) & (key_pos[None, :] >= 0)
    scores = jnp.where(inside[None], scores, neg_fill)
    row_max = jnp.max(scores, axis=2, keepdims=True)
    expo = jnp.exp(scores - row_max)
    attend = expo / jnp.sum(expo, axis=2, keepdims=True)
    attend_low = attend.astype(jnp.bfloat16)
    dprob = jnp.einsum("trd,jd->rtj", h_heads, value_rows, preferred_element_type=jnp.float32)
    row_delta = jnp.sum(attend * dprob, axis=2, keepdims=True)
    dscore = (attend * (dprob - row_delta)).astype(jnp.bfloat16)
    key_part = (
        jnp.einsum("rtj,trd->jd", dscore, q_heads, preferred_element_type=jnp.float32) * factor
    )
    value_part = jnp.einsum("rtj,trd->jd", attend_low, h_heads, preferred_element_type=jnp.float32)
    return (key_part, value_part)


def linear_terms(q_block, h_block, key_rows, value_rows, log_rates, lin_scale):
    head_dim = key_rows.shape[1]
    group_size = q_block.shape[1] // head_dim
    length = q_block.shape[0]
    q_heads = q_block.reshape(length, group_size, head_dim)
    h_heads = h_block.reshape(length, group_size, head_dim)
    log_sums = jnp.cumsum(log_rates)
    row_after = lax.broadcasted_iota(jnp.int32, (length, length), 0)
    row_before = lax.broadcasted_iota(jnp.int32, (length, length), 1)
    mixing = jnp.exp(
        jnp.where(row_after >= row_before, log_sums[:, None] - log_sums[None, :], neg_fill)
    )
    key_mix = (
        mixing[None]
        * jnp.einsum("trd,jd->rtj", h_heads, value_rows, preferred_element_type=jnp.float32)
    ).astype(jnp.bfloat16)
    value_mix = (
        mixing[None]
        * jnp.einsum("trd,jd->rtj", q_heads, key_rows, preferred_element_type=jnp.float32)
    ).astype(jnp.bfloat16)
    key_part = (
        jnp.einsum("rtj,trd->jd", key_mix, q_heads, preferred_element_type=jnp.float32) * lin_scale
    )
    value_part = (
        jnp.einsum("rtj,trd->jd", value_mix, h_heads, preferred_element_type=jnp.float32)
        * lin_scale
    )
    weighted = (jnp.exp(log_sums)[:, None, None] * h_heads).astype(jnp.bfloat16)
    block_grad = (
        jnp.einsum("trd,tre->de", q_heads, weighted, preferred_element_type=jnp.float32) * lin_scale
    )
    return (
        key_part,
        value_part,
        block_grad,
        jnp.exp(log_sums[-1]),
        jnp.exp(log_sums[-1] - log_sums),
    )


def compose(earlier, later):
    return (later[0] * earlier[0], later[0][:, None, None] * earlier[1] + later[1])


def on_device(layer_input, queries, keys, values, result_cotangent, log_decay):
    length = queries.shape[0]
    head_dim = E
    lin_scale = 1.0 / (32 * head_dim)
    halves = result_cotangent * 0.5
    row_start = lax.axis_index("ctx") * length
    query_pos = row_start + jnp.arange(length, dtype=jnp.int32)
    key_pos = row_start - WINDOW + jnp.arange(length + WINDOW, dtype=jnp.int32)
    linear_parts = [linear_terms(queries, halves, keys, values, log_decay[0], lin_scale)]
    decays = jnp.stack([part[3] for part in linear_parts])
    block_grads = jnp.stack([part[2] for part in linear_parts])
    identity = (jnp.ones_like(decays), jnp.zeros_like(block_grads))
    _, incoming = entering((decays, block_grads), "ctx", compose, identity)
    preceding_keys, prior_v = shifted((keys, values), "ctx", 1)
    full_k = jnp.concatenate([preceding_keys, keys], axis=0)
    full_v = jnp.concatenate([prior_v, values], axis=0)
    band_parts = [band_grads(queries, halves, full_k, full_v, query_pos, key_pos)]
    win_k = jnp.concatenate([part[0] for part in band_parts], axis=1)
    win_v = jnp.concatenate([part[1] for part in band_parts], axis=1)
    back_k, back_v = shifted((win_k[:WINDOW], win_v[:WINDOW]), "ctx", -1)
    win_k = win_k[WINDOW:]
    win_v = win_v[WINDOW:]
    zero_rows = jnp.zeros((length - WINDOW, win_k.shape[1]), jnp.float32)
    win_k = win_k + jnp.concatenate([zero_rows, back_k], axis=0)
    win_v = win_v + jnp.concatenate([zero_rows, back_v], axis=0)
    state_in = incoming[0]
    tail_decay = linear_parts[0][4][:, None]
    lin_keys = linear_parts[0][0] + tail_decay * jnp.dot(
        values.astype(jnp.float32), state_in.T, precision=lax.Precision.HIGHEST
    )
    lin_values = linear_parts[0][1] + tail_decay * jnp.dot(
        keys.astype(jnp.float32), state_in, precision=lax.Precision.HIGHEST
    )
    key_grad = (lin_keys + win_k).astype(jnp.bfloat16)
    value_grad = (lin_values + win_v).astype(jnp.bfloat16)
    both_grads = jnp.concatenate([key_grad, value_grad], axis=1)
    partial_value = lax.dot_general(
        lax.all_gather(layer_input, "head", axis=1, tiled=True),
        both_grads,
        (((0,), (0,)), ((), ())),
        preferred_element_type=jnp.float32,
    )
    owned = lax.psum_scatter(partial_value, "ctx", scatter_dimension=0, tiled=True)
    key_width = key_grad.shape[1]
    return (owned[:, :key_width].astype(jnp.bfloat16), owned[:, key_width:].astype(jnp.bfloat16))


def solution(mesh):
    in_specs = (
        P("ctx", "head"),
        P("ctx", "head"),
        P("ctx", "head"),
        P("ctx", "head"),
        P("ctx", "head"),
        P("head", "ctx"),
    )
    out_specs = (P("ctx", "head"), P("ctx", "head"))
    return jax.shard_map(
        on_device, mesh=mesh, in_specs=in_specs, out_specs=out_specs, check_vma=False
    )
```

profile of v0, /device:TPU:0, one launch (start us, length us, event | category | flops | bytes accessed | tf_op | source)
XLA Modules:
  0.0 181.2 jit_solution(12835178251088065102)
XLA Ops:
  7.2 4.9 %collective-permute-start = (bf16[256,128]{1,0:T(8,128)(2,1)}, bf16[256,128]{1,0:T(8,128)(2,1)S(1)}, u32[]{:S(2)}, u32[]{:S(2)}) collective-permute-start(bf16[256,128]{1,0:T(8,128)(2,1)} %param.10), channel_id=1, source_target_pairs={{0,4},{4,8},{8,12},{12,16},{16,20},{20,24},{24,28},{1,5},{5,9},{9,... | collective-permute-start | bytes 196616 | tf_op jit(solution)/shard_map/ppermute | solution.py:34
  12.1 3.4 %collective-permute-start.1 = (bf16[256,128]{1,0:T(8,128)(2,1)}, bf16[256,128]{1,0:T(8,128)(2,1)S(1)}, u32[]{:S(2)}, u32[]{:S(2)}) collective-permute-start(bf16[256,128]{1,0:T(8,128)(2,1)} %param.11), channel_id=1, source_target_pairs={{0,4},{4,8},{8,12},{12,16},{16,20},{20,24},{24,28},{1,5},{5,9},{9,... | collective-permute-start | bytes 196616 | tf_op jit(solution)/shard_map/ppermute | solution.py:34
  15.7 1.0 reduce-window.9
  19.0 1.0 copy.35
  20.0 0.9 broadcast_multiply_fusion
  21.1 1.1 fusion.45
  22.4 31.3 %all-gather = f32[1024,128]{0,1:T(8,128)S(1)} all-gather(f32[128,128]{0,1:T(8,128)S(1)} %fusion.18), channel_id=2, replica_groups=mesh['ctx'=8,'head'=4] {'ctx'}, dimensions={0}, use_global_device_ids=true | all-gather | bytes 589824 | tf_op jit(solution)/shard_map/all_gather | solution.py:15
  54.3 0.8 dynamic-update-slice
  55.2 19.4 %all-reduce = f32[8]{0:T(128)S(1)} all-reduce(f32[8]{0:T(128)S(1)} %dynamic-update-slice), channel_id=1, replica_groups=mesh['ctx'=8,'head'=4] {'ctx'}, use_global_device_ids=true, to_apply=%add | all-reduce | flops 8 | bytes 64
  74.6 11.2 %while.16 = (s32[]{:T(128)}, f32[1,128,128]{2,1,0:T(8,128)S(1)}, s32[]{:T(128)}, f32[8,1]{0,1:T(1,128)S(1)}, f32[8,1,128,128]{3,2,1,0:T(8,128)S(1)}, /*index=5*/s32[]{:T(128)}, s32[]{:T(128)}, s32[]{:T(128)}, s32[]{:T(128)}) while((s32[]{:T(128)}, f32[1,128,128]{2,1,0:T(8,128)S(1)}, s32[]{:T(128)}, f32[8,1]{0,1:T(1,128)S(1)}, ...), condition=%wide.region_3.4_spmd.clone, body=%wide.region_2.3_spmd.clone.sunk | while | flops 65544 | bytes 196787 | solution.py:28
  75.3 0.7 fusion.75
  76.7 0.7 fusion.75
  87.8 0.7 convolution_bitcast_fusion.3
  88.6 1.3 collective-permute-start.3
  89.9 1.3 multiply_reduce_fusion
  91.1 2.0 %fusion.9 = f32[512,128]{0,1:T(8,128)S(1)} fusion(bf16[256,2,128]{0,2,1:T(8,128)(2,1)S(1)} %bitcast.144, f32[2,256,512]{1,2,0:T(8,128)} %get-tuple-element.184, f32[2,256]{1,0:T(2,128)S(1)} %get-tuple-element.183, f32[2,256]{1,0:T(2,128)S(1)} %get-tuple-element.181, pred[256,512]{0,1:T(8,128)(4,1)S(1)} %fusion.23, bf16[256,128]{1,0:T(8,128)(2,1)S(1)} %copy-done, ...), kind=kOutput, calls=%fused_computation.17 | convolution fusion | flops 136381440 | bytes 1708032 | tf_op jit(solution)/shard_map/rtj,trd->jd/dot_general | solution.py:58
  93.2 1.3 collective-permute-start.2
  94.5 1.0 collective-permute-done.3
  95.7 5.0 %collective-permute-done.2 = f32[256,128]{0,1:T(8,128)S(1)} collective-permute-done((f32[256,128]{0,1:T(8,128)S(1)}, f32[256,128]{0,1:T(8,128)S(1)}, u32[]{:S(2)}, u32[]{:S(2)}) %collective-permute-start.2) | collective-permute-done | bytes 131104 | tf_op jit(solution)/shard_map/ppermute | solution.py:34
  100.9 3.0 %convolution_bitcast_fusion = f32[2048,256]{0,1:T(8,128)} fusion(bf16[256,2048]{1,0:T(8,128)(2,1)} %all-gather.3.cloned.1.call-done, bf16[256,128]{0,1:T(8,128)(2,1)S(1)} %fusion.28, bf16[256,128]{0,1:T(8,128)(2,1)S(1)} %fusion.30), kind=kOutput, calls=%fused_computation.4 | convolution fusion | flops 268697600 | bytes 3276800 | tf_op jit(solution)/shard_map/dot_general | solution.py:144
  103.9 68.0 %reduce-scatter.2.cloned.1.call-done = f32[256,256]{0,1:T(8,128)} async-done(((f32[2048,256]{0,1:T(8,128)}), f32[256,256]{0,1:T(8,128)}) %reduce-scatter.2.cloned.1.call-update) | async-done | bytes 262160 | tf_op jit(solution)/shard_map/reduce_scatter | solution.py:150
  171.9 1.0 convert.4
  172.9 0.7 copy.28
  173.6 0.7 copy.29
  (53 shorter events, 14.9 us)
Async XLA Ops:
  7.2 46.5 %copy-start.2 = (u32[32]{0:T(128)S(1)}, u32[32]{0:T(128)}, u32[]{:S(2)}) copy-start(u32[32]{0:T(128)} %constant.78) | copy-start | bytes 388
  7.2 93.7 %all-gather.3.cloned.1.call-start = ((), (), s32[]{:S(2)}) async-start(), calls=%async_computation.1 | async-start | bytes 1310720 | tf_op jit(solution)/shard_map/all_gather | solution.py:145
  7.2 80.1 %collective-permute-start = (bf16[256,128]{1,0:T(8,128)(2,1)}, bf16[256,128]{1,0:T(8,128)(2,1)S(1)}, u32[]{:S(2)}, u32[]{:S(2)}) collective-permute-start(bf16[256,128]{1,0:T(8,128)(2,1)} %param.10), channel_id=1, source_target_pairs={{0,4},{4,8},{8,12},{12,16},{16,20},{20,24},{24,28},{1,5},{5,9},{9,... | collective-permute-start | bytes 196616 | tf_op jit(solution)/shard_map/ppermute | solution.py:34
  12.1 77.8 %collective-permute-start.1 = (bf16[256,128]{1,0:T(8,128)(2,1)}, bf16[256,128]{1,0:T(8,128)(2,1)S(1)}, u32[]{:S(2)}, u32[]{:S(2)}) collective-permute-start(bf16[256,128]{1,0:T(8,128)(2,1)} %param.11), channel_id=1, source_target_pairs={{0,4},{4,8},{8,12},{12,16},{16,20},{20,24},{24,28},{1,5},{5,9},{9,... | collective-permute-start | bytes 196616 | tf_op jit(solution)/shard_map/ppermute | solution.py:34
  15.6 156.3 %reduce-scatter.2.cloned.1.call-start = ((), (), s32[]{:S(2)}) async-start(), calls=%async_computation.2 | async-start | bytes 2359296 | tf_op jit(solution)/shard_map/reduce_scatter | solution.py:150
  21.0 64.8 %copy-start = (bf16[256,128]{1,0:T(8,128)(2,1)S(1)}, bf16[256,128]{1,0:T(8,128)(2,1)}, u32[]{:S(2)}) copy-start(bf16[256,128]{1,0:T(8,128)(2,1)} %param.10) | copy-start | bytes 196612
  53.7 33.1 %copy-start.1 = (bf16[256,128]{1,0:T(8,128)(2,1)S(1)}, bf16[256,128]{1,0:T(8,128)(2,1)}, u32[]{:S(2)}) copy-start(bf16[256,128]{1,0:T(8,128)(2,1)} %param.11) | copy-start | bytes 196612
  88.6 6.9 %collective-permute-start.3 = (f32[256,128]{0,1:T(8,128)S(1)}, f32[256,128]{0,1:T(8,128)S(1)}, u32[]{:S(2)}, u32[]{:S(2)}) collective-permute-start(f32[256,128]{0,1:T(8,128)S(1)} %slice.43), channel_id=1, source_target_pairs={{4,0},{8,4},{12,8},{16,12},{20,16},{24,20},{28,24},{5,1},{9,5},{13... | collective-permute-start | bytes 393224 | tf_op jit(solution)/shard_map/ppermute | solution.py:34
  93.2 7.5 %collective-permute-start.2 = (f32[256,128]{0,1:T(8,128)S(1)}, f32[256,128]{0,1:T(8,128)S(1)}, u32[]{:S(2)}, u32[]{:S(2)}) collective-permute-start(f32[256,128]{0,1:T(8,128)S(1)} %slice.41), channel_id=1, source_target_pairs={{4,0},{8,4},{12,8},{16,12},{20,16},{24,20},{28,24},{5,1},{9,5},{13... | collective-permute-start | bytes 393224 | tf_op jit(solution)/shard_map/ppermute | solution.py:34
Sparse Core Ops, SparseCore 0:
  15.7 16.9 all-gather.2
  104.0 67.8 reduce-scatter.1
where the time goes:
time: 182 us; the launch traced here: 181 us
  waiting for transfers between devices  74 us (41%)
  blocking collectives  50.7 us (28%)
  between operations  15 us (8%)
  starting transfers between devices  11 us (6%)
  local copies, waits for them, and re-layouts  10.2 us (6%)
  other arithmetic  10.1 us (6%)
  matrix products  9.95 us (5%)
    reduce_scatter x1, waiting for transfers between devices, on_device(): lax.psum_scatter(partial_value, 'ctx', scatter_dimension=0, tiled=True)  68 us
    all_gather x1, blocking collectives, entering(): everything = jax.tree.map(lambda part: lax.all_gather(part, axis), array)  31.3 us
    unnamed x1, blocking collectives  19.4 us
    ppermute x4, starting transfers between devices, shifted(): lax.ppermute(value, axis, [(source, source + steps) for source in range(l...  10.9 us
    ppermute x4, waiting for transfers between devices, shifted(): lax.ppermute(value, axis, [(source, source + steps) for source in range(l...  5.92 us
    select_n x8, other arithmetic, turn(): return jax.tree.map(lambda a, b: jnp.where(reached, a, b), new, before)  5.63 us
    dynamic_slice x8, local copies, waits for them, and re-layouts, turn(): new = combine(before, jax.tree.map(lambda part: part[at], everything))  5.32 us
  transfers between devices with their start and end apart: 6, of which 3 were waited for; matrix products, arithmetic and copies ran while one was open for 14% of the time, Pallas kernels for 0%

commit v1 on v0

--- a/solution.py
+++ b/solution.py
@@ -1,6 +1,10 @@
+import functools
+
 import jax
 import jax.numpy as jnp
 from jax import lax
+from jax.experimental import pallas as pl
+from jax.experimental.pallas import tpu as pltpu
 from jax.sharding import PartitionSpec as P
 
 E = 128
@@ -67,9 +71,9 @@
     length = q_block.shape[0]
     q_heads = q_block.reshape(length, group_size, head_dim)
     h_heads = h_block.reshape(length, group_size, head_dim)
-    log_sums = jnp.cumsum(log_rates)
     row_after = lax.broadcasted_iota(jnp.int32, (length, length), 0)
     row_before = lax.broadcasted_iota(jnp.int32, (length, length), 1)
+    log_sums = jnp.sum(jnp.where(row_after >= row_before, log_rates[None, :], 0.0), axis=1)
     mixing = jnp.exp(
         jnp.where(row_after >= row_before, log_sums[:, None] - log_sums[None, :], neg_fill)
     )
@@ -152,6 +156,330 @@
     return (owned[:, :key_width].astype(jnp.bfloat16), owned[:, key_width:].astype(jnp.bfloat16))
 
 
+MESH = pl.DeviceIdType.MESH
+F32, BF16 = jnp.float32, jnp.bfloat16
+
+
+def fits(args, n, heads):
+    x, q, k = args[0], args[1], args[2]
+    rows = x.shape[1] * heads // n
+    return (
+        heads == 4
+        and n == 2 * heads
+        and rows % 128 == 0
+        and x.shape[0] == WINDOW
+        and k.shape[1] == E
+        and q.shape[1] % E == 0
+        and x.shape[1] == 2 * rows
+    )
+
+
+def tn(a, b):
+    return lax.dot_general(a, b, (((0,), (0,)), ((), ())), preferred_element_type=F32)
+
+
+def nt(a, b):
+    return lax.dot_general(a, b, (((1,), (1,)), ((), ())), preferred_element_type=F32)
+
+
+def fused_kernel(
+    n, m, x_ref, q_ref, k_ref, v_ref, d_ref, ld_ref, ok_ref, ov_ref,
+    xall, gall, sall, halo, back_out, back_in, part_k, part_v, state,
+    x_send, x_recv, f_send, g_send, g_recv, s_send, s_recv, h_send, h_recv, b_send, b_recv,
+):
+    length, width = q_ref.shape
+    group = width // E
+    rows = x_ref.shape[1] // m
+    factor = E ** (-0.5)
+    lin_scale = 1.0 / (32 * E)
+    c, h = lax.axis_index("ctx"), lax.axis_index("head")
+    owner = c // m
+    sibling = h + 1 - 2 * lax.rem(h, 2)
+    across = lax.rem(h + 2, 4)
+
+    def copy(src, dst, send, recv, ctx, head):
+        return pltpu.make_async_remote_copy(
+            src_ref=src, dst_ref=dst, send_sem=send, recv_sem=recv,
+            device_id=(ctx, head), device_id_type=MESH,
+        )
+
+    peers = [lax.rem(c + i, n) for i in range(1, n)]
+    barrier = pltpu.get_barrier_semaphore()
+    for p in peers:
+        pl.semaphore_signal(barrier, inc=1, device_id=(p, h), device_id_type=MESH)
+    for i in range(1, 4):
+        pl.semaphore_signal(
+            barrier, inc=1, device_id=(c, lax.rem(h + i, 4)), device_id_type=MESH
+        )
+    pl.semaphore_wait(barrier, n + 2)
+
+    def halo_copy(i):
+        return copy(
+            (k_ref, v_ref)[i], halo.at[i], h_send.at[i], h_recv.at[i], lax.rem(c + 1, n), h
+        )
+
+    @pl.when(c < n - 1)
+    def _():
+        halo_copy(0).start()
+        halo_copy(1).start()
+
+    @pl.when(c == 0)
+    def _():
+        halo[...] = jnp.zeros_like(halo)
+
+    def x_copy(j):
+        return copy(
+            x_ref.at[:, j * rows : (j + 1) * rows], xall.at[c],
+            x_send.at[j], x_recv.at[c], h * m + j, h,
+        )
+
+    for j in range(m):
+
+        @pl.when(h * m + j == c)
+        def _():
+            xall[c] = x_ref[:, j * rows : (j + 1) * rows]
+
+        @pl.when(h * m + j != c)
+        def _():
+            x_copy(j).start()
+
+    after = lax.broadcasted_iota(jnp.int32, (length, length), 0)
+    before = lax.broadcasted_iota(jnp.int32, (length, length), 1)
+    lower = after >= before
+    sums = jnp.sum(jnp.where(lower, ld_ref[...], 0.0), axis=1, keepdims=True)
+    sums_row = jnp.sum(jnp.where(after == before, sums, 0.0), axis=0, keepdims=True)
+    total = jnp.sum(ld_ref[...], axis=1, keepdims=True)
+
+    grown = jnp.exp(sums)
+    qs, hs, grad = [], [], jnp.zeros((E, E), F32)
+    for r in range(group):
+        qs.append(q_ref[:, r * E : (r + 1) * E])
+        hs.append((d_ref[:, r * E : (r + 1) * E].astype(F32) * 0.5).astype(BF16))
+        grad += tn(qs[r], (grown * hs[r].astype(F32)).astype(BF16))
+    decay = jnp.broadcast_to(jnp.exp(total), (16, E))
+    coarse = decay.astype(BF16)
+    fine = (decay - coarse.astype(F32)).astype(BF16)
+    sall[c, 0:E, :] = (grad * lin_scale).astype(BF16)
+    sall[c, E : E + 16, :] = coarse
+    sall[c, E + 16 : E + 32, :] = fine
+
+    def state_copy(i):
+        return copy(
+            sall.at[c], sall.at[c], s_send.at[i], s_recv.at[c], lax.rem(c + n - i, n), h
+        )
+
+    for i in range(1, n):
+
+        @pl.when(c - i >= 0)
+        def _():
+            state_copy(i).start()
+
+    mixing = jnp.exp(jnp.where(lower, sums - sums_row, neg_fill))
+    keys, vals = k_ref[...], v_ref[...]
+    lin_k = jnp.zeros((length, E), F32)
+    lin_v = jnp.zeros((length, E), F32)
+    own_s, own_p = [], []
+    for r in range(group):
+        own_s.append(nt(qs[r], keys))
+        own_p.append(nt(hs[r], vals))
+        lin_k += tn((mixing * own_p[r]).astype(BF16), qs[r])
+        lin_v += tn((mixing * own_s[r]).astype(BF16), hs[r])
+
+    @pl.when(c > 0)
+    def _():
+        halo_copy(0).wait_recv()
+        halo_copy(1).wait_recv()
+
+    old_k, old_v = halo[0], halo[1]
+    upper = jnp.logical_and(before > after, c > 0)
+    win = [jnp.zeros((length, E), F32) for _ in range(4)]
+    for r in range(group):
+        s_own = jnp.where(lower, own_s[r] * factor, neg_fill)
+        s_old = jnp.where(upper, nt(qs[r], old_k) * factor, neg_fill)
+        top = jnp.maximum(
+            jnp.max(s_own, axis=1, keepdims=True), jnp.max(s_old, axis=1, keepdims=True)
+        )
+        e_own, e_old = jnp.exp(s_own - top), jnp.exp(s_old - top)
+        inv = 1.0 / (jnp.sum(e_own, axis=1, keepdims=True) + jnp.sum(e_old, axis=1, keepdims=True))
+        a_own, a_old = e_own * inv, e_old * inv
+        p_old = nt(hs[r], old_v)
+        delta = jnp.sum(a_own * own_p[r], axis=1, keepdims=True) + jnp.sum(
+            a_old * p_old, axis=1, keepdims=True
+        )
+        win[0] += tn((a_old * (p_old - delta)).astype(BF16), qs[r])
+        win[1] += tn(a_old.astype(BF16), hs[r])
+        win[2] += tn((a_own * (own_p[r] - delta)).astype(BF16), qs[r])
+        win[3] += tn(a_own.astype(BF16), hs[r])
+    back_out[0] = (win[0] * factor).astype(BF16)
+    back_out[1] = win[1].astype(BF16)
+
+    def back_copy(i):
+        return copy(
+            back_out.at[i], back_in.at[i], b_send.at[i], b_recv.at[i], lax.rem(c + n - 1, n), h
+        )
+
+    @pl.when(c > 0)
+    def _():
+        back_copy(0).start()
+        back_copy(1).start()
+
+    part_k[...] = lin_k * lin_scale + win[2] * factor
+    part_v[...] = lin_v * lin_scale + win[3]
+
+    def forward(slot, i, head):
+        return copy(xall.at[slot], xall.at[slot], f_send.at[i], x_recv.at[slot], c, head)
+
+    def arrived(slot):
+        return copy(xall.at[slot], xall.at[slot], x_send.at[0], x_recv.at[slot], c, sibling)
+
+    @pl.when(h == owner)
+    def _():
+        for i in range(n):
+            slot = lax.rem(c + i, n)
+            if i:
+                arrived(slot).wait_recv()
+            forward(slot, 2 * i, across).start()
+            forward(slot, 2 * i + 1, sibling).start()
+
+    state[...] = jnp.zeros_like(state)
+    for i in range(n - 1, 0, -1):
+
+        @pl.when(c + i < n)
+        def _():
+            slot = lax.rem(c + i, n)
+            copy(
+                sall.at[slot], sall.at[slot], s_send.at[0], s_recv.at[slot], slot, h
+            ).wait_recv()
+            kept = sall[slot, E : E + 1, :].astype(F32) + sall[slot, E + 16 : E + 17, :].astype(F32)
+            state[...] = kept * state[...] + sall[slot, 0:E, :].astype(F32)
+
+    high = state[...].astype(BF16)
+    low = (state[...] - high.astype(F32)).astype(BF16)
+    ending = jnp.exp(total - sums)
+    part_k[...] += ending * (nt(vals, high) + nt(vals, low))
+    part_v[...] += ending * (
+        jnp.dot(keys, high, preferred_element_type=F32)
+        + jnp.dot(keys, low, preferred_element_type=F32)
+    )
+
+    @pl.when(c < n - 1)
+    def _():
+        back_copy(0).wait_recv()
+        back_copy(1).wait_recv()
+        part_k[...] += back_in[0].astype(F32)
+        part_v[...] += back_in[1].astype(F32)
+
+    gall[c, :, 0:E] = part_k[...].astype(BF16)
+    gall[c, :, E : 2 * E] = part_v[...].astype(BF16)
+
+    def g_copy(i):
+        return copy(gall.at[c], gall.at[c], g_send.at[i], g_recv.at[c], lax.rem(c + i, n), h)
+
+    for i in range(1, n):
+        g_copy(i).start()
+
+    @pl.when(across == owner)
+    def _():
+        for i in range(n):
+            slot = lax.rem(c + i, n)
+            arrived(slot).wait_recv()
+            forward(slot, i, sibling).start()
+
+    @pl.when(lax.rem(h + owner, 2) == 1)
+    def _():
+        for i in range(n):
+            arrived(lax.rem(c + i, n)).wait_recv()
+
+    acc = jnp.zeros((rows, 2 * E), F32)
+    for i in range(n):
+        slot = lax.rem(c + i, n)
+        if i:
+            copy(
+                gall.at[slot], gall.at[slot], g_send.at[0], g_recv.at[slot], slot, h
+            ).wait_recv()
+        acc += tn(xall[slot], gall[slot])
+    ok_ref[...] = acc[:, 0:E].astype(BF16)
+    ov_ref[...] = acc[:, E : 2 * E].astype(BF16)
+
+    @pl.when(c < n - 1)
+    def _():
+        halo_copy(0).wait_send()
+        halo_copy(1).wait_send()
+
+    @pl.when(c > 0)
+    def _():
+        back_copy(0).wait_send()
+        back_copy(1).wait_send()
+
+    for j in range(m):
+
+        @pl.when(h * m + j != c)
+        def _():
+            x_copy(j).wait_send()
+
+    for i in range(1, n):
+
+        @pl.when(c - i >= 0)
+        def _():
+            state_copy(i).wait_send()
+
+    @pl.when(h == owner)
+    def _():
+        for i in range(n):
+            slot = lax.rem(c + i, n)
+            forward(slot, 2 * i, across).wait_send()
+            forward(slot, 2 * i + 1, sibling).wait_send()
+
+    @pl.when(across == owner)
+    def _():
+        for i in range(n):
+            forward(lax.rem(c + i, n), i, sibling).wait_send()
+
+    for i in range(1, n):
+        g_copy(i).wait_send()
+
+
+def fused(layer_input, queries, keys, values, result_cotangent, log_decay):
+    n = lax.axis_size("ctx")
+    length, width = layer_input.shape
+    rows = width * lax.axis_size("head") // n
+    m = width // rows
+    dma = pltpu.SemaphoreType.DMA
+    shape = jax.ShapeDtypeStruct((rows, E), BF16)
+    vmem = pl.BlockSpec(memory_space=pltpu.VMEM)
+    return pl.pallas_call(
+        functools.partial(fused_kernel, n, m),
+        out_shape=(shape, shape),
+        in_specs=[vmem] * 6,
+        out_specs=(vmem, vmem),
+        scratch_shapes=[
+            pltpu.VMEM((n, length, rows), BF16),
+            pltpu.VMEM((n, length, 2 * E), BF16),
+            pltpu.VMEM((n, E + 32, E), BF16),
+            pltpu.VMEM((2, length, E), BF16),
+            pltpu.VMEM((2, length, E), BF16),
+            pltpu.VMEM((2, length, E), BF16),
+            pltpu.VMEM((length, E), F32),
+            pltpu.VMEM((length, E), F32),
+            pltpu.VMEM((E, E), F32),
+            dma((m,)),
+            dma((n,)),
+            dma((2 * n,)),
+            dma((2 * n,)),
+            dma((2 * n,)),
+            dma((n,)),
+            dma((n,)),
+            dma((2,)),
+            dma((2,)),
+            dma((2,)),
+            dma((2,)),
+        ],
+        compiler_params=pltpu.CompilerParams(
+            collective_id=0, has_side_effects=True, vmem_limit_bytes=32 * 1024 * 1024
+        ),
+    )(layer_input, queries, keys, values, result_cotangent, log_decay)
+
+
 def solution(mesh):
     in_specs = (
         P("ctx", "head"),
@@ -162,6 +490,11 @@
         P("head", "ctx"),
     )
     out_specs = (P("ctx", "head"), P("ctx", "head"))
+    n, heads = mesh.shape["ctx"], mesh.shape["head"]
+
+    def body(*args):
+        return (fused if fits(args, n, heads) else on_device)(*args)
+
     return jax.shard_map(
-        on_device, mesh=mesh, in_specs=in_specs, out_specs=out_specs, check_vma=False
-    )
+        body, mesh=mesh, in_specs=in_specs, out_specs=out_specs, check_vma=False
+    )

time: 182 us -> 68.6 us (0.38)
  the two profiles are of different devices: /device:TPU:0 before, /device:TPU:28 now
where the time goes in v1:
time: 68.6 us; the launch traced here: 68.3 us
  Pallas kernels  61.3 us (89%)
  local copies, waits for them, and re-layouts  6.37 us (9%)
    pallas_call x1, Pallas kernels, fused(): pl.pallas_call(functools.partial(fused_kernel, n, m), out_shape=(shape, s...  61.3 us
    unnamed x14, local copies, waits for them, and re-layouts  6.37 us

profile of v1, /device:TPU:28, one launch (start us, length us, event | category | flops | bytes accessed | tf_op | source)
XLA Modules:
  0.0 68.3 jit_solution(3995464031096614796)
XLA Ops:
  0.6 0.0 copy-start
  0.6 0.9 %copy-done = bf16[256,512]{1,0:T(8,128)(2,1)S(1)} copy-done((bf16[256,512]{1,0:T(8,128)(2,1)S(1)}, bf16[256,512]{1,0:T(8,128)(2,1)}, u32[]{:S(2)}) %copy-start) | copy-done | bytes 262168
  1.6 0.0 copy-start.1
  1.6 0.9 %copy-done.1 = bf16[256,256]{1,0:T(8,128)(2,1)S(1)} copy-done((bf16[256,256]{1,0:T(8,128)(2,1)S(1)}, bf16[256,256]{1,0:T(8,128)(2,1)}, u32[]{:S(2)}) %copy-start.1) | copy-done | bytes 131096
  2.5 0.0 copy-start.2
  2.5 0.9 %copy-done.2 = bf16[256,256]{1,0:T(8,128)(2,1)S(1)} copy-done((bf16[256,256]{1,0:T(8,128)(2,1)S(1)}, bf16[256,256]{1,0:T(8,128)(2,1)}, u32[]{:S(2)}) %copy-start.2) | copy-done | bytes 131096
  3.4 0.0 copy-start.3
  3.4 0.8 %copy-done.3 = bf16[256,128]{1,0:T(8,128)(2,1)S(1)} copy-done((bf16[256,128]{1,0:T(8,128)(2,1)S(1)}, bf16[256,128]{1,0:T(8,128)(2,1)}, u32[]{:S(2)}) %copy-start.3) | copy-done | bytes 65560
  4.2 0.0 copy-start.4
  4.2 0.8 %copy-done.4 = bf16[256,128]{1,0:T(8,128)(2,1)S(1)} copy-done((bf16[256,128]{1,0:T(8,128)(2,1)S(1)}, bf16[256,128]{1,0:T(8,128)(2,1)}, u32[]{:S(2)}) %copy-start.4) | copy-done | bytes 65560
  5.1 0.0 copy-start.5
  5.1 0.7 copy-done.5
  5.8 61.3 %shard_map.77 = (bf16[256,128]{1,0:T(8,128)(2,1)S(1)}, bf16[256,128]{1,0:T(8,128)(2,1)S(1)}) custom-call(bf16[256,512]{1,0:T(8,128)(2,1)S(1)} %copy-done, bf16[256,256]{1,0:T(8,128)(2,1)S(1)} %copy-done.1, bf16[256,128]{1,0:T(8,128)(2,1)S(1)} %copy-done.3, bf16[256,128]{1,0:T(8,128)(2,1)S(1)} %copy-done.4, bf16[256,256]{1,0:T(8,128)(2,1)S(1)} %copy-done.2, ...), custom_call_target="tpu_custom_call" | custom-call | tf_op jit(solution)/shard_map/pallas_call | solution.py:450
  67.1 0.6 copy.10
  67.7 0.6 copy.11
Async XLA Ops:
  0.6 1.0 %copy-start = (bf16[256,512]{1,0:T(8,128)(2,1)S(1)}, bf16[256,512]{1,0:T(8,128)(2,1)}, u32[]{:S(2)}) copy-start(bf16[256,512]{1,0:T(8,128)(2,1)} %x_ref.1) | copy-start | bytes 786436
  1.6 0.9 %copy-start.1 = (bf16[256,256]{1,0:T(8,128)(2,1)S(1)}, bf16[256,256]{1,0:T(8,128)(2,1)}, u32[]{:S(2)}) copy-start(bf16[256,256]{1,0:T(8,128)(2,1)} %q_ref.1) | copy-start | bytes 393220
  2.5 0.9 %copy-start.2 = (bf16[256,256]{1,0:T(8,128)(2,1)S(1)}, bf16[256,256]{1,0:T(8,128)(2,1)}, u32[]{:S(2)}) copy-start(bf16[256,256]{1,0:T(8,128)(2,1)} %d_ref.1) | copy-start | bytes 393220
  3.4 0.8 %copy-start.3 = (bf16[256,128]{1,0:T(8,128)(2,1)S(1)}, bf16[256,128]{1,0:T(8,128)(2,1)}, u32[]{:S(2)}) copy-start(bf16[256,128]{1,0:T(8,128)(2,1)} %k_ref.1) | copy-start | bytes 196612
  4.2 0.8 %copy-start.4 = (bf16[256,128]{1,0:T(8,128)(2,1)S(1)}, bf16[256,128]{1,0:T(8,128)(2,1)}, u32[]{:S(2)}) copy-start(bf16[256,128]{1,0:T(8,128)(2,1)} %v_ref.1) | copy-start | bytes 196612
  5.1 0.7 copy-start.5

commit v2 on v1

--- a/solution.py
+++ b/solution.py
@@ -183,13 +183,14 @@
 
 
 def fused_kernel(
-    n, m, x_ref, q_ref, k_ref, v_ref, d_ref, ld_ref, ok_ref, ov_ref,
-    xall, gall, sall, halo, back_out, back_in, part_k, part_v, state,
-    x_send, x_recv, f_send, g_send, g_recv, s_send, s_recv, h_send, h_recv, b_send, b_recv,
+    n, m, x_ref, q_hbm, k_hbm, v_hbm, d_hbm, ld_hbm, ok_ref, ov_ref,
+    q_ref, k_ref, v_ref, d_ref, ld_ref, in_sem, xall, gall, sall, halo, back_out, back_in, part_k, part_v, state,
+    x_send, x_recv, x_own, f_send, g_up, g_down, g_side, g_recv, s_send, s_recv, h_send, h_recv, b_send, b_recv,
 ):
     length, width = q_ref.shape
     group = width // E
     rows = x_ref.shape[1] // m
+    part = length // 2
     factor = E ** (-0.5)
     lin_scale = 1.0 / (32 * E)
     c, h = lax.axis_index("ctx"), lax.axis_index("head")
@@ -203,19 +204,29 @@
             device_id=(ctx, head), device_id_type=MESH,
         )
 
+    loads = [
+        pltpu.make_async_copy(src, dst, in_sem.at[i])
+        for i, (src, dst) in enumerate(
+            ((ld_hbm, ld_ref), (q_hbm, q_ref), (d_hbm, d_ref), (k_hbm, k_ref), (v_hbm, v_ref))
+        )
+    ]
+    for load in loads:
+        load.start()
+
     peers = [lax.rem(c + i, n) for i in range(1, n)]
     barrier = pltpu.get_barrier_semaphore()
     for p in peers:
         pl.semaphore_signal(barrier, inc=1, device_id=(p, h), device_id_type=MESH)
+        pl.semaphore_signal(barrier, inc=1, device_id=(p, across), device_id_type=MESH)
     for i in range(1, 4):
         pl.semaphore_signal(
             barrier, inc=1, device_id=(c, lax.rem(h + i, 4)), device_id_type=MESH
         )
-    pl.semaphore_wait(barrier, n + 2)
+    pl.semaphore_wait(barrier, 2 * n + 1)
 
     def halo_copy(i):
         return copy(
-            (k_ref, v_ref)[i], halo.at[i], h_send.at[i], h_recv.at[i], lax.rem(c + 1, n), h
+            (k_hbm, v_hbm)[i], halo.at[i], h_send.at[i], h_recv.at[i], lax.rem(c + 1, n), h
         )
 
     @pl.when(c < n - 1)
@@ -227,21 +238,31 @@
     def _():
         halo[...] = jnp.zeros_like(halo)
 
-    def x_copy(j):
+    def x_copy(j, p):
         return copy(
-            x_ref.at[:, j * rows : (j + 1) * rows], xall.at[c],
-            x_send.at[j], x_recv.at[c], h * m + j, h,
+            x_ref.at[pl.ds(p * part, part), pl.ds(j * rows, rows)], xall.at[p, c],
+            x_send.at[j, p], x_recv.at[p, c], h * m + j, (h, across)[p],
+        )
+
+    def x_local(j):
+        return pltpu.make_async_copy(
+            x_ref.at[pl.ds(0, part), pl.ds(j * rows, rows)], xall.at[0, c], x_own
         )
 
     for j in range(m):
 
         @pl.when(h * m + j == c)
         def _():
-            xall[c] = x_ref[:, j * rows : (j + 1) * rows]
+            x_local(j).start()
 
         @pl.when(h * m + j != c)
         def _():
-            x_copy(j).start()
+            x_copy(j, 0).start()
+
+        x_copy(j, 1).start()
+
+    for load in loads:
+        load.wait()
 
     after = lax.broadcasted_iota(jnp.int32, (length, length), 0)
     before = lax.broadcasted_iota(jnp.int32, (length, length), 1)
@@ -326,20 +347,27 @@
     part_k[...] = lin_k * lin_scale + win[2] * factor
     part_v[...] = lin_v * lin_scale + win[3]
 
-    def forward(slot, i, head):
-        return copy(xall.at[slot], xall.at[slot], f_send.at[i], x_recv.at[slot], c, head)
-
-    def arrived(slot):
-        return copy(xall.at[slot], xall.at[slot], x_send.at[0], x_recv.at[slot], c, sibling)
-
-    @pl.when(h == owner)
-    def _():
-        for i in range(n):
-            slot = lax.rem(c + i, n)
-            if i:
-                arrived(slot).wait_recv()
-            forward(slot, 2 * i, across).start()
-            forward(slot, 2 * i + 1, sibling).start()
+    def forward(p, slot, i, head):
+        return copy(xall.at[p, slot], xall.at[p, slot], f_send.at[i], x_recv.at[p, slot], c, head)
+
+    def arrived(p, slot):
+        return copy(
+            xall.at[p, slot], xall.at[p, slot], x_send.at[0, 0], x_recv.at[p, slot], c, sibling
+        )
+
+    roots = (h == owner, across == owner)
+    for p in range(2):
+
+        @pl.when(roots[p])
+        def _():
+            for i in range(n - 1, -1, -1):
+                slot = lax.rem(c + i, n)
+                if i or p:
+                    arrived(p, slot).wait_recv()
+                else:
+                    x_local(0).wait()
+                forward(p, slot, 3 * i, across).start()
+                forward(p, slot, 3 * i + 1, sibling).start()
 
     state[...] = jnp.zeros_like(state)
     for i in range(n - 1, 0, -1):
@@ -369,37 +397,99 @@
         part_k[...] += back_in[0].astype(F32)
         part_v[...] += back_in[1].astype(F32)
 
-    gall[c, :, 0:E] = part_k[...].astype(BF16)
-    gall[c, :, E : 2 * E] = part_v[...].astype(BF16)
-
-    def g_copy(i):
-        return copy(gall.at[c], gall.at[c], g_send.at[i], g_recv.at[c], lax.rem(c + i, n), h)
-
-    for i in range(1, n):
-        g_copy(i).start()
-
-    @pl.when(across == owner)
-    def _():
-        for i in range(n):
-            slot = lax.rem(c + i, n)
-            arrived(slot).wait_recv()
-            forward(slot, i, sibling).start()
+    gall[0, c] = part_k[...].astype(BF16)
+    gall[1, c] = part_v[...].astype(BF16)
+
+    side = c + 1 - 2 * lax.rem(c, 2)
+    up_ok, down_ok = c < n - 2, c >= 2
+
+    def up(p, slot):
+        return copy(gall.at[p, slot], gall.at[p, slot], g_up.at[p, slot], g_recv.at[p, slot], lax.rem(c + 2, n), h)
+
+    def down(p, slot):
+        return copy(gall.at[p, slot], gall.at[p, slot], g_down.at[p, slot], g_recv.at[p, slot], lax.rem(c + n - 2, n), h)
+
+    def beside(p, slot):
+        return copy(gall.at[p, slot], gall.at[p, slot], g_side.at[p, slot], g_recv.at[p, slot], side, h)
+
+    def along(act, p, slot, upward, downward):
+        if upward:
+
+            @pl.when(up_ok)
+            def _():
+                act(up(p, slot))
+
+        if downward:
+
+            @pl.when(down_ok)
+            def _():
+                act(down(p, slot))
+
+    def start(dma):
+        dma.start()
+
+    def sent(dma):
+        dma.wait_send()
+
+    def arrive(p, slot):
+        beside(p, slot).wait_recv()
+
+    def spread(act, wait):
+        act(beside(0, c))
+        along(act, 0, c, True, True)
+        along(act, 1, c, True, True)
+        act(beside(1, c))
+        if wait:
+            arrive(0, side)
+        along(act, 0, side, True, True)
+        for d in range(2, n, 2):
+
+            @pl.when(c - d >= 0)
+            def _():
+                for p, slot in ((0, c - d), (1, c - d), (0, side - d)):
+                    if wait:
+                        arrive(p, slot)
+                    along(act, p, slot, True, False)
+                    if p:
+                        act(beside(p, slot))
+
+            @pl.when(c + d < n)
+            def _():
+                for p, slot in ((0, c + d), (1, c + d), (0, side + d)):
+                    if wait:
+                        arrive(p, slot)
+                    along(act, p, slot, False, True)
+                    if p:
+                        act(beside(p, slot))
+
+    spread(start, True)
+
+    for p in range(2):
+
+        @pl.when(roots[1 - p])
+        def _():
+            for i in range(n - 1, -1, -1):
+                slot = lax.rem(c + i, n)
+                arrived(p, slot).wait_recv()
+                forward(p, slot, 3 * i + 2, sibling).start()
 
     @pl.when(lax.rem(h + owner, 2) == 1)
     def _():
-        for i in range(n):
-            arrived(lax.rem(c + i, n)).wait_recv()
-
-    acc = jnp.zeros((rows, 2 * E), F32)
-    for i in range(n):
-        slot = lax.rem(c + i, n)
-        if i:
-            copy(
-                gall.at[slot], gall.at[slot], g_send.at[0], g_recv.at[slot], slot, h
-            ).wait_recv()
-        acc += tn(xall[slot], gall[slot])
-    ok_ref[...] = acc[:, 0:E].astype(BF16)
-    ov_ref[...] = acc[:, E : 2 * E].astype(BF16)
+        for slot in range(n):
+            arrived(0, slot).wait_recv()
+            arrived(1, slot).wait_recv()
+
+    for i in range(0, n, 2):
+        slot = lax.rem(side + i, n)
+        arrive(1, slot)
+    acc_k = jnp.zeros((rows, E), F32)
+    acc_v = jnp.zeros((rows, E), F32)
+    for slot in range(n):
+        both = xall[:, slot].reshape(length, rows)
+        acc_k += tn(both, gall[0, slot])
+        acc_v += tn(both, gall[1, slot])
+    ok_ref[...] = acc_k.astype(BF16)
+    ov_ref[...] = acc_v.astype(BF16)
 
     @pl.when(c < n - 1)
     def _():
@@ -415,7 +505,9 @@
 
         @pl.when(h * m + j != c)
         def _():
-            x_copy(j).wait_send()
+            x_copy(j, 0).wait_send()
+
+        x_copy(j, 1).wait_send()
 
     for i in range(1, n):
 
@@ -423,20 +515,17 @@
         def _():
             state_copy(i).wait_send()
 
-    @pl.when(h == owner)
-    def _():
-        for i in range(n):
-            slot = lax.rem(c + i, n)
-            forward(slot, 2 * i, across).wait_send()
-            forward(slot, 2 * i + 1, sibling).wait_send()
-
-    @pl.when(across == owner)
-    def _():
-        for i in range(n):
-            forward(lax.rem(c + i, n), i, sibling).wait_send()
-
-    for i in range(1, n):
-        g_copy(i).wait_send()
+    for p in range(2):
+
+        @pl.when(roots[p])
+        def _():
+            for i in range(n):
+                slot = lax.rem(c + i, n)
+                forward(p, slot, 3 * i, across).wait_send()
+                forward(p, slot, 3 * i + 1, sibling).wait_send()
+                forward(1 - p, slot, 3 * i + 2, sibling).wait_send()
+
+    spread(sent, False)
 
 
 def fused(layer_input, queries, keys, values, result_cotangent, log_decay):
@@ -450,11 +539,17 @@
     return pl.pallas_call(
         functools.partial(fused_kernel, n, m),
         out_shape=(shape, shape),
-        in_specs=[vmem] * 6,
+        in_specs=[pl.BlockSpec(memory_space=pltpu.HBM)] * 6,
         out_specs=(vmem, vmem),
         scratch_shapes=[
-            pltpu.VMEM((n, length, rows), BF16),
-            pltpu.VMEM((n, length, 2 * E), BF16),
+            pltpu.VMEM(queries.shape, BF16),
+            pltpu.VMEM(keys.shape, BF16),
+            pltpu.VMEM(values.shape, BF16),
+            pltpu.VMEM(queries.shape, BF16),
+            pltpu.VMEM(log_decay.shape, F32),
+            dma((5,)),
+            pltpu.VMEM((2, n, length // 2, rows), BF16),
+            pltpu.VMEM((2, n, length, E), BF16),
             pltpu.VMEM((n, E + 32, E), BF16),
             pltpu.VMEM((2, length, E), BF16),
             pltpu.VMEM((2, length, E), BF16),
@@ -462,11 +557,14 @@
             pltpu.VMEM((length, E), F32),
             pltpu.VMEM((length, E), F32),
             pltpu.VMEM((E, E), F32),
-            dma((m,)),
-            dma((n,)),
-            dma((2 * n,)),
-            dma((2 * n,)),
-            dma((2 * n,)),
+            dma((m, 2)),
+            dma((2, n)),
+            dma,
+            dma((3 * n,)),
+            dma((2, n)),
+            dma((2, n)),
+            dma((2, n)),
+            dma((2, n)),
             dma((n,)),
             dma((n,)),
             dma((2,)),

time: 68.6 us -> 56.4 us (0.82)
  the two profiles are of different devices: /device:TPU:28 before, /device:TPU:0 now
where the time goes in v2:
time: 56.4 us; the launch traced here: 56 us
  Pallas kernels  49 us (87%)
  local copies, waits for them, and re-layouts  6.37 us (11%)
  between operations  0.65 us (1%)
    pallas_call x1, Pallas kernels, fused(): pl.pallas_call(functools.partial(fused_kernel, n, m), out_shape=(shape, s...  49 us
    unnamed x14, local copies, waits for them, and re-layouts  6.37 us

profile of v2, /device:TPU:0, one launch (start us, length us, event | category | flops | bytes accessed | tf_op | source)
XLA Modules:
  0.0 56.0 jit_solution(9909563053016710018)
XLA Ops:
  0.6 0.0 copy-start
  0.6 0.9 %copy-done = bf16[256,512]{1,0:T(8,128)(2,1)S(1)} copy-done((bf16[256,512]{1,0:T(8,128)(2,1)S(1)}, bf16[256,512]{1,0:T(8,128)(2,1)}, u32[]{:S(2)}) %copy-start) | copy-done | bytes 262168
  1.6 0.0 copy-start.1
  1.6 0.9 %copy-done.1 = bf16[256,256]{1,0:T(8,128)(2,1)S(1)} copy-done((bf16[256,256]{1,0:T(8,128)(2,1)S(1)}, bf16[256,256]{1,0:T(8,128)(2,1)}, u32[]{:S(2)}) %copy-start.1) | copy-done | bytes 131096
  2.5 0.0 copy-start.2
  2.5 0.9 %copy-done.2 = bf16[256,256]{1,0:T(8,128)(2,1)S(1)} copy-done((bf16[256,256]{1,0:T(8,128)(2,1)S(1)}, bf16[256,256]{1,0:T(8,128)(2,1)}, u32[]{:S(2)}) %copy-start.2) | copy-done | bytes 131096
  3.4 0.0 copy-start.3
  3.4 0.8 %copy-done.3 = bf16[256,128]{1,0:T(8,128)(2,1)S(1)} copy-done((bf16[256,128]{1,0:T(8,128)(2,1)S(1)}, bf16[256,128]{1,0:T(8,128)(2,1)}, u32[]{:S(2)}) %copy-start.3) | copy-done | bytes 65560
  4.2 0.0 copy-start.4
  4.2 0.8 %copy-done.4 = bf16[256,128]{1,0:T(8,128)(2,1)S(1)} copy-done((bf16[256,128]{1,0:T(8,128)(2,1)S(1)}, bf16[256,128]{1,0:T(8,128)(2,1)}, u32[]{:S(2)}) %copy-start.4) | copy-done | bytes 65560
  5.1 0.0 copy-start.5
  5.1 0.7 %copy-done.5 = f32[1,256]{1,0:T(1,128)S(1)} copy-done((f32[1,256]{1,0:T(1,128)S(1)}, f32[1,256]{1,0:T(1,128)}, u32[]{:S(2)}) %copy-start.5) | copy-done | bytes 1048
  5.8 49.0 %shard_map.77 = (bf16[256,128]{1,0:T(8,128)(2,1)S(1)}, bf16[256,128]{1,0:T(8,128)(2,1)S(1)}) custom-call(bf16[256,512]{1,0:T(8,128)(2,1)S(1)} %copy-done, bf16[256,256]{1,0:T(8,128)(2,1)S(1)} %copy-done.1, bf16[256,128]{1,0:T(8,128)(2,1)S(1)} %copy-done.3, bf16[256,128]{1,0:T(8,128)(2,1)S(1)} %copy-done.4, bf16[256,256]{1,0:T(8,128)(2,1)S(1)} %copy-done.2, ...), custom_call_target="tpu_custom_call" | custom-call | tf_op jit(solution)/shard_map/pallas_call | solution.py:539
  54.8 0.6 %copy.10 = bf16[256,128]{1,0:T(8,128)(2,1)} copy(bf16[256,128]{1,0:T(8,128)(2,1)S(1)} %get-tuple-element.4) | data formatting | bytes 131072
  55.4 0.6 %copy.11 = bf16[256,128]{1,0:T(8,128)(2,1)} copy(bf16[256,128]{1,0:T(8,128)(2,1)S(1)} %get-tuple-element.5) | data formatting | bytes 131072
Async XLA Ops:
  0.6 1.0 %copy-start = (bf16[256,512]{1,0:T(8,128)(2,1)S(1)}, bf16[256,512]{1,0:T(8,128)(2,1)}, u32[]{:S(2)}) copy-start(bf16[256,512]{1,0:T(8,128)(2,1)} %x_ref.1) | copy-start | bytes 786436
  1.6 0.9 %copy-start.1 = (bf16[256,256]{1,0:T(8,128)(2,1)S(1)}, bf16[256,256]{1,0:T(8,128)(2,1)}, u32[]{:S(2)}) copy-start(bf16[256,256]{1,0:T(8,128)(2,1)} %q_hbm.1) | copy-start | bytes 393220
  2.5 0.9 %copy-start.2 = (bf16[256,256]{1,0:T(8,128)(2,1)S(1)}, bf16[256,256]{1,0:T(8,128)(2,1)}, u32[]{:S(2)}) copy-start(bf16[256,256]{1,0:T(8,128)(2,1)} %d_hbm.1) | copy-start | bytes 393220
  3.4 0.8 %copy-start.3 = (bf16[256,128]{1,0:T(8,128)(2,1)S(1)}, bf16[256,128]{1,0:T(8,128)(2,1)}, u32[]{:S(2)}) copy-start(bf16[256,128]{1,0:T(8,128)(2,1)} %k_hbm.1) | copy-start | bytes 196612
  4.2 0.8 %copy-start.4 = (bf16[256,128]{1,0:T(8,128)(2,1)S(1)}, bf16[256,128]{1,0:T(8,128)(2,1)}, u32[]{:S(2)}) copy-start(bf16[256,128]{1,0:T(8,128)(2,1)} %v_hbm.1) | copy-start | bytes 196612
  5.1 0.7 %copy-start.5 = (f32[1,256]{1,0:T(1,128)S(1)}, f32[1,256]{1,0:T(1,128)}, u32[]{:S(2)}) copy-start(f32[1,256]{1,0:T(1,128)} %ld_hbm.1) | copy-start | bytes 3076

commit v3 on v2

--- a/solution.py
+++ b/solution.py
@@ -184,7 +184,7 @@
 
 def fused_kernel(
     n, m, x_ref, q_hbm, k_hbm, v_hbm, d_hbm, ld_hbm, ok_ref, ov_ref,
-    q_ref, k_ref, v_ref, d_ref, ld_ref, in_sem, xall, gall, sall, halo, back_out, back_in, part_k, part_v, state,
+    q_ref, k_ref, v_ref, d_ref, ld_ref, in_sem, xall, gall, sall, halo, back_out, back_in, part_k, part_v, state, chain_out, chain_in,
     x_send, x_recv, x_own, f_send, g_up, g_down, g_side, g_recv, s_send, s_recv, h_send, h_recv, b_send, b_recv,
 ):
     length, width = q_ref.shape
@@ -284,16 +284,12 @@
     sall[c, E : E + 16, :] = coarse
     sall[c, E + 16 : E + 32, :] = fine
 
-    def state_copy(i):
-        return copy(
-            sall.at[c], sall.at[c], s_send.at[i], s_recv.at[c], lax.rem(c + n - i, n), h
-        )
-
-    for i in range(1, n):
-
-        @pl.when(c - i >= 0)
-        def _():
-            state_copy(i).start()
+    side = c + 1 - 2 * lax.rem(c, 2)
+
+    def state_copy():
+        return copy(sall.at[c], sall.at[c], s_send.at[0], s_recv.at[c], side, h)
+
+    state_copy().start()
 
     mixing = jnp.exp(jnp.where(lower, sums - sums_row, neg_fill))
     keys, vals = k_ref[...], v_ref[...]
@@ -356,6 +352,118 @@
         )
 
     roots = (h == owner, across == owner)
+    def chain():
+        return copy(chain_out, chain_in, s_send.at[1], s_recv.at[n], lax.rem(c + n - 2, n), h)
+
+    copy(sall.at[side], sall.at[side], s_send.at[0], s_recv.at[side], side, h).wait_recv()
+
+    @pl.when(c >= n - 2)
+    def _():
+        chain_in[...] = jnp.zeros_like(chain_in)
+
+    @pl.when(c < n - 2)
+    def _():
+        chain().wait_recv()
+
+    def through(slot, later):
+        kept = sall[slot, E : E + 1, :].astype(F32) + sall[slot, E + 16 : E + 17, :].astype(F32)
+        return kept * later + sall[slot, 0:E, :].astype(F32)
+
+    first = c - lax.rem(c, 2)
+    beyond = chain_in[...]
+    between = through(first + 1, beyond)
+
+    @pl.when(c >= 2)
+    def _():
+        chain_out[...] = through(first, between)
+        chain().start()
+
+    state[...] = jnp.where(c == first, between, beyond)
+
+    high = state[...].astype(BF16)
+    low = (state[...] - high.astype(F32)).astype(BF16)
+    ending = jnp.exp(total - sums)
+    part_k[...] += ending * (nt(vals, high) + nt(vals, low))
+    part_v[...] += ending * (
+        jnp.dot(keys, high, preferred_element_type=F32)
+        + jnp.dot(keys, low, preferred_element_type=F32)
+    )
+
+    @pl.when(c < n - 1)
+    def _():
+        back_copy(0).wait_recv()
+        back_copy(1).wait_recv()
+        part_k[...] += back_in[0].astype(F32)
+        part_v[...] += back_in[1].astype(F32)
+
+    gall[0, c] = part_k[...].astype(BF16)
+    gall[1, c] = part_v[...].astype(BF16)
+
+    up_ok, down_ok = c < n - 2, c >= 2
+
+    def up(p, slot):
+        return copy(gall.at[p, slot], gall.at[p, slot], g_up.at[p, slot], g_recv.at[p, slot], lax.rem(c + 2, n), h)
+
+    def down(p, slot):
+        return copy(gall.at[p, slot], gall.at[p, slot], g_down.at[p, slot], g_recv.at[p, slot], lax.rem(c + n - 2, n), h)
+
+    def beside(p, slot):
+        return copy(gall.at[p, slot], gall.at[p, slot], g_side.at[p, slot], g_recv.at[p, slot], side, h)
+
+    def along(act, p, slot, upward, downward):
+        if upward:
+
+            @pl.when(up_ok)
+            def _():
+                act(up(p, slot))
+
+        if downward:
+
+            @pl.when(down_ok)
+            def _():
+                act(down(p, slot))
+
+    def start(dma):
+        dma.start()
+
+    def sent(dma):
+        dma.wait_send()
+
+    def arrive(p, slot):
+        beside(p, slot).wait_recv()
+
+    def share(act):
+        act(beside(0, c))
+        along(act, 0, c, True, True)
+        along(act, 1, c, True, True)
+        act(beside(1, c))
+
+    def spread(act, wait):
+        if wait:
+            arrive(0, side)
+        along(act, 0, side, True, True)
+        for d in range(2, n, 2):
+
+            @pl.when(c - d >= 0)
+            def _():
+                for p, slot in ((0, c - d), (1, c - d), (0, side - d)):
+                    if wait:
+                        arrive(p, slot)
+                    along(act, p, slot, True, False)
+                    if p:
+                        act(beside(p, slot))
+
+            @pl.when(c + d < n)
+            def _():
+                for p, slot in ((0, c + d), (1, c + d), (0, side + d)):
+                    if wait:
+                        arrive(p, slot)
+                    along(act, p, slot, False, True)
+                    if p:
+                        act(beside(p, slot))
+
+    share(start)
+
     for p in range(2):
 
         @pl.when(roots[p])
@@ -368,99 +476,6 @@
                     x_local(0).wait()
                 forward(p, slot, 3 * i, across).start()
                 forward(p, slot, 3 * i + 1, sibling).start()
-
-    state[...] = jnp.zeros_like(state)
-    for i in range(n - 1, 0, -1):
-
-        @pl.when(c + i < n)
-        def _():
-            slot = lax.rem(c + i, n)
-            copy(
-                sall.at[slot], sall.at[slot], s_send.at[0], s_recv.at[slot], slot, h
-            ).wait_recv()
-            kept = sall[slot, E : E + 1, :].astype(F32) + sall[slot, E + 16 : E + 17, :].astype(F32)
-            state[...] = kept * state[...] + sall[slot, 0:E, :].astype(F32)
-
-    high = state[...].astype(BF16)
-    low = (state[...] - high.astype(F32)).astype(BF16)
-    ending = jnp.exp(total - sums)
-    part_k[...] += ending * (nt(vals, high) + nt(vals, low))
-    part_v[...] += ending * (
-        jnp.dot(keys, high, preferred_element_type=F32)
-        + jnp.dot(keys, low, preferred_element_type=F32)
-    )
-
-    @pl.when(c < n - 1)
-    def _():
-        back_copy(0).wait_recv()
-        back_copy(1).wait_recv()
-        part_k[...] += back_in[0].astype(F32)
-        part_v[...] += back_in[1].astype(F32)
-
-    gall[0, c] = part_k[...].astype(BF16)
-    gall[1, c] = part_v[...].astype(BF16)
-
-    side = c + 1 - 2 * lax.rem(c, 2)
-    up_ok, down_ok = c < n - 2, c >= 2
-
-    def up(p, slot):
-        return copy(gall.at[p, slot], gall.at[p, slot], g_up.at[p, slot], g_recv.at[p, slot], lax.rem(c + 2, n), h)
-
-    def down(p, slot):
-        return copy(gall.at[p, slot], gall.at[p, slot], g_down.at[p, slot], g_recv.at[p, slot], lax.rem(c + n - 2, n), h)
-
-    def beside(p, slot):
-        return copy(gall.at[p, slot], gall.at[p, slot], g_side.at[p, slot], g_recv.at[p, slot], side, h)
-
-    def along(act, p, slot, upward, downward):
-        if upward:
-
-            @pl.when(up_ok)
-            def _():
-                act(up(p, slot))
-
-        if downward:
-
-            @pl.when(down_ok)
-            def _():
-                act(down(p, slot))
-
-    def start(dma):
-        dma.start()
-
-    def sent(dma):
-        dma.wait_send()
-
-    def arrive(p, slot):
-        beside(p, slot).wait_recv()
-
-    def spread(act, wait):
-        act(beside(0, c))
-        along(act, 0, c, True, True)
-        along(act, 1, c, True, True)
-        act(beside(1, c))
-        if wait:
-            arrive(0, side)
-        along(act, 0, side, True, True)
-        for d in range(2, n, 2):
-
-            @pl.when(c - d >= 0)
-            def _():
-                for p, slot in ((0, c - d), (1, c - d), (0, side - d)):
-                    if wait:
-                        arrive(p, slot)
-                    along(act, p, slot, True, False)
-                    if p:
-                        act(beside(p, slot))
-
-            @pl.when(c + d < n)
-            def _():
-                for p, slot in ((0, c + d), (1, c + d), (0, side + d)):
-                    if wait:
-                        arrive(p, slot)
-                    along(act, p, slot, False, True)
-                    if p:
-                        act(beside(p, slot))
 
     spread(start, True)
 
@@ -509,11 +524,11 @@
 
         x_copy(j, 1).wait_send()
 
-    for i in range(1, n):
-
-        @pl.when(c - i >= 0)
-        def _():
-            state_copy(i).wait_send()
+    state_copy().wait_send()
+
+    @pl.when(c >= 2)
+    def _():
+        chain().wait_send()
 
     for p in range(2):
 
@@ -525,6 +540,7 @@
                 forward(p, slot, 3 * i + 1, sibling).wait_send()
                 forward(1 - p, slot, 3 * i + 2, sibling).wait_send()
 
+    share(sent)
     spread(sent, False)
 
 
@@ -557,6 +573,8 @@
             pltpu.VMEM((length, E), F32),
             pltpu.VMEM((length, E), F32),
             pltpu.VMEM((E, E), F32),
+            pltpu.VMEM((E, E), F32),
+            pltpu.VMEM((E, E), F32),
             dma((m, 2)),
             dma((2, n)),
             dma,
@@ -565,15 +583,15 @@
             dma((2, n)),
             dma((2, n)),
             dma((2, n)),
-            dma((n,)),
-            dma((n,)),
+            dma((2,)),
+            dma((n + 1,)),
             dma((2,)),
             dma((2,)),
             dma((2,)),
             dma((2,)),
         ],
         compiler_params=pltpu.CompilerParams(
-            collective_id=0, has_side_effects=True, vmem_limit_bytes=32 * 1024 * 1024
+            collective_id=0, has_side_effects=True, vmem_limit_bytes=60 * 1024 * 1024
         ),
     )(layer_input, queries, keys, values, result_cotangent, log_decay)
 

time: 56.4 us -> 49.5 us (0.88)
  local copies, waits for them, and re-layouts: 6.37 us -> 2.14 us
  Pallas kernels: 49 us -> 46.5 us
    unnamed x14 -> x4, local copies, waits for them, and re-layouts: 6.37 us -> 2.14 us
    pallas_call x1, Pallas kernels: 49 us -> 46.5 us  [fused(): pl.pallas_call(functools.partial(fused_kernel, n, m), out_shape=(shape, s...]
where the time goes in v3:
time: 49.5 us; the launch traced here: 49.3 us
  Pallas kernels  46.5 us (94%)
  local copies, waits for them, and re-layouts  2.14 us (4%)
  between operations  0.65 us (1%)
    pallas_call x1, Pallas kernels, fused(): pl.pallas_call(functools.partial(fused_kernel, n, m), out_shape=(shape, s...  46.5 us
    unnamed x4, local copies, waits for them, and re-layouts  2.14 us

profile of v3, /device:TPU:0, one launch (start us, length us, event | category | flops | bytes accessed | tf_op | source)
XLA Modules:
  0.0 49.3 jit_solution(13312761043462527093)
XLA Ops:
  0.6 46.5 %shard_map.77 = (bf16[256,128]{1,0:T(8,128)(2,1)}, bf16[256,128]{1,0:T(8,128)(2,1)}) custom-call(bf16[256,512]{1,0:T(8,128)(2,1)} %x_ref.1, bf16[256,256]{1,0:T(8,128)(2,1)} %q_hbm.1, bf16[256,128]{1,0:T(8,128)(2,1)} %k_hbm.1, bf16[256,128]{1,0:T(8,128)(2,1)} %v_hbm.1, bf16[256,256]{1,0:T(8,128)(2,1)} %d_hbm.1, f32[1,256]{1,0:T(1,128)} %ld_hbm.1), custom_call_target="tpu_custom_call" | custom-call | tf_op jit(solution)/shard_map/pallas_call | solution.py:555
  47.2 0.0 copy-start
  47.2 1.5 %copy.10 = bf16[256,128]{1,0:T(8,128)(2,1)} copy(bf16[256,128]{1,0:T(8,128)(2,1)} %get-tuple-element.4) | data formatting | bytes 131072
  48.7 0.0 copy-done
  48.7 0.6 %copy.11 = bf16[256,128]{1,0:T(8,128)(2,1)} copy(bf16[256,128]{1,0:T(8,128)(2,1)S(1)} %copy-done) | data formatting | bytes 131072
Async XLA Ops:
  47.2 1.5 %copy-start = (bf16[256,128]{1,0:T(8,128)(2,1)S(1)}, bf16[256,128]{1,0:T(8,128)(2,1)}, u32[]{:S(2)}) copy-start(bf16[256,128]{1,0:T(8,128)(2,1)} %get-tuple-element.5) | copy-start | bytes 196612

commit v4 on v3

--- a/solution.py
+++ b/solution.py
@@ -302,6 +302,39 @@
         lin_k += tn((mixing * own_p[r]).astype(BF16), qs[r])
         lin_v += tn((mixing * own_s[r]).astype(BF16), hs[r])
 
+    def chain():
+        return copy(chain_out, chain_in, s_send.at[1], s_recv.at[n], lax.rem(c + n - 2, n), h)
+
+    def enter():
+        copy(sall.at[side], sall.at[side], s_send.at[0], s_recv.at[side], side, h).wait_recv()
+
+        @pl.when(c >= n - 2)
+        def _():
+            chain_in[...] = jnp.zeros_like(chain_in)
+
+        @pl.when(c < n - 2)
+        def _():
+            chain().wait_recv()
+
+        def through(slot, later):
+            kept = sall[slot, E : E + 1, :].astype(F32) + sall[slot, E + 16 : E + 17, :].astype(F32)
+            return kept * later + sall[slot, 0:E, :].astype(F32)
+
+        first = c - lax.rem(c, 2)
+        beyond = chain_in[...].astype(F32)
+        between = through(first + 1, beyond)
+
+        @pl.when(c >= 2)
+        def _():
+            chain_out[...] = through(first, between).astype(BF16)
+            chain().start()
+
+        state[...] = jnp.where(c == first, between, beyond)
+
+    @pl.when(c >= n // 2)
+    def _():
+        enter()
+
     @pl.when(c > 0)
     def _():
         halo_copy(0).wait_recv()
@@ -352,33 +385,9 @@
         )
 
     roots = (h == owner, across == owner)
-    def chain():
-        return copy(chain_out, chain_in, s_send.at[1], s_recv.at[n], lax.rem(c + n - 2, n), h)
-
-    copy(sall.at[side], sall.at[side], s_send.at[0], s_recv.at[side], side, h).wait_recv()
-
-    @pl.when(c >= n - 2)
-    def _():
-        chain_in[...] = jnp.zeros_like(chain_in)
-
-    @pl.when(c < n - 2)
-    def _():
-        chain().wait_recv()
-
-    def through(slot, later):
-        kept = sall[slot, E : E + 1, :].astype(F32) + sall[slot, E + 16 : E + 17, :].astype(F32)
-        return kept * later + sall[slot, 0:E, :].astype(F32)
-
-    first = c - lax.rem(c, 2)
-    beyond = chain_in[...]
-    between = through(first + 1, beyond)
-
-    @pl.when(c >= 2)
-    def _():
-        chain_out[...] = through(first, between)
-        chain().start()
-
-    state[...] = jnp.where(c == first, between, beyond)
+    @pl.when(c < n // 2)
+    def _():
+        enter()
 
     high = state[...].astype(BF16)
     low = (state[...] - high.astype(F32)).astype(BF16)
@@ -573,8 +582,8 @@
             pltpu.VMEM((length, E), F32),
             pltpu.VMEM((length, E), F32),
             pltpu.VMEM((E, E), F32),
-            pltpu.VMEM((E, E), F32),
-            pltpu.VMEM((E, E), F32),
+            pltpu.VMEM((E, E), BF16),
+            pltpu.VMEM((E, E), BF16),
             dma((m, 2)),
             dma((2, n)),
             dma,

time: 49.5 us -> 47.3 us (0.956)
  Pallas kernels: 46.5 us -> 44.3 us
    pallas_call x1, Pallas kernels: 46.5 us -> 44.3 us  [fused(): pl.pallas_call(functools.partial(fused_kernel, n, m), out_shape=(shape, s...]
where the time goes in v4:
time: 47.3 us; the launch traced here: 47.1 us
  Pallas kernels  44.3 us (94%)
  local copies, waits for them, and re-layouts  2.14 us (5%)
  between operations  0.65 us (1%)
    pallas_call x1, Pallas kernels, fused(): pl.pallas_call(functools.partial(fused_kernel, n, m), out_shape=(shape, s...  44.3 us
    unnamed x4, local copies, waits for them, and re-layouts  2.14 us

profile of v4, /device:TPU:0, one launch (start us, length us, event | category | flops | bytes accessed | tf_op | source)
XLA Modules:
  0.0 47.1 jit_solution(9760449135328370340)
XLA Ops:
  0.6 44.3 %shard_map.77 = (bf16[256,128]{1,0:T(8,128)(2,1)}, bf16[256,128]{1,0:T(8,128)(2,1)}) custom-call(bf16[256,512]{1,0:T(8,128)(2,1)} %x_ref.1, bf16[256,256]{1,0:T(8,128)(2,1)} %q_hbm.1, bf16[256,128]{1,0:T(8,128)(2,1)} %k_hbm.1, bf16[256,128]{1,0:T(8,128)(2,1)} %v_hbm.1, bf16[256,256]{1,0:T(8,128)(2,1)} %d_hbm.1, f32[1,256]{1,0:T(1,128)} %ld_hbm.1), custom_call_target="tpu_custom_call" | custom-call | tf_op jit(solution)/shard_map/pallas_call | solution.py:564
  45.0 0.0 copy-start
  45.0 1.5 %copy.10 = bf16[256,128]{1,0:T(8,128)(2,1)} copy(bf16[256,128]{1,0:T(8,128)(2,1)} %get-tuple-element.4) | data formatting | bytes 131072
  46.5 0.0 copy-done
  46.5 0.6 %copy.11 = bf16[256,128]{1,0:T(8,128)(2,1)} copy(bf16[256,128]{1,0:T(8,128)(2,1)S(1)} %copy-done) | data formatting | bytes 131072
Async XLA Ops:
  45.0 1.5 %copy-start = (bf16[256,128]{1,0:T(8,128)(2,1)S(1)}, bf16[256,128]{1,0:T(8,128)(2,1)}, u32[]{:S(2)}) copy-start(bf16[256,128]{1,0:T(8,128)(2,1)} %get-tuple-element.5) | copy-start | bytes 196612

commit v5 on v4

--- a/solution.py
+++ b/solution.py
@@ -447,11 +447,23 @@
         along(act, 1, c, True, True)
         act(beside(1, c))
 
+    def hand_on():
+        for p in range(2):
+
+            @pl.when(roots[1 - p])
+            def _():
+                for i in range(n - 1, -1, -1):
+                    slot = lax.rem(c + i, n)
+                    arrived(p, slot).wait_recv()
+                    forward(p, slot, 3 * i + 2, sibling).start()
+
     def spread(act, wait):
         if wait:
             arrive(0, side)
         along(act, 0, side, True, True)
         for d in range(2, n, 2):
+            if wait and d == 4:
+                hand_on()
 
             @pl.when(c - d >= 0)
             def _():
@@ -487,15 +499,6 @@
                 forward(p, slot, 3 * i + 1, sibling).start()
 
     spread(start, True)
-
-    for p in range(2):
-
-        @pl.when(roots[1 - p])
-        def _():
-            for i in range(n - 1, -1, -1):
-                slot = lax.rem(c + i, n)
-                arrived(p, slot).wait_recv()
-                forward(p, slot, 3 * i + 2, sibling).start()
 
     @pl.when(lax.rem(h + owner, 2) == 1)
     def _():

time: 47.3 us -> 47.3 us (level)
  no operation moved by 1% of the time
where the time goes in v5:
time: 47.3 us; the launch traced here: 47.1 us
  Pallas kernels  44.3 us (94%)
  local copies, waits for them, and re-layouts  2.14 us (5%)
  between operations  0.65 us (1%)
    pallas_call x1, Pallas kernels, fused(): pl.pallas_call(functools.partial(fused_kernel, n, m), out_shape=(shape, s...  44.3 us
    unnamed x4, local copies, waits for them, and re-layouts  2.14 us

profile of v5, /device:TPU:0, one launch (start us, length us, event | category | flops | bytes accessed | tf_op | source)
XLA Modules:
  0.0 47.1 jit_solution(872238867149892125)
XLA Ops:
  0.6 44.3 %shard_map.77 = (bf16[256,128]{1,0:T(8,128)(2,1)}, bf16[256,128]{1,0:T(8,128)(2,1)}) custom-call(bf16[256,512]{1,0:T(8,128)(2,1)} %x_ref.1, bf16[256,256]{1,0:T(8,128)(2,1)} %q_hbm.1, bf16[256,128]{1,0:T(8,128)(2,1)} %k_hbm.1, bf16[256,128]{1,0:T(8,128)(2,1)} %v_hbm.1, bf16[256,256]{1,0:T(8,128)(2,1)} %d_hbm.1, f32[1,256]{1,0:T(1,128)} %ld_hbm.1), custom_call_target="tpu_custom_call" | custom-call | tf_op jit(solution)/shard_map/pallas_call | solution.py:567
  45.0 0.0 copy-start
  45.0 1.5 %copy.10 = bf16[256,128]{1,0:T(8,128)(2,1)} copy(bf16[256,128]{1,0:T(8,128)(2,1)} %get-tuple-element.4) | data formatting | bytes 131072
  46.5 0.0 copy-done
  46.5 0.6 %copy.11 = bf16[256,128]{1,0:T(8,128)(2,1)} copy(bf16[256,128]{1,0:T(8,128)(2,1)S(1)} %copy-done) | data formatting | bytes 131072
Async XLA Ops:
  45.0 1.5 %copy-start = (bf16[256,128]{1,0:T(8,128)(2,1)S(1)}, bf16[256,128]{1,0:T(8,128)(2,1)}, u32[]{:S(2)}) copy-start(bf16[256,128]{1,0:T(8,128)(2,1)} %get-tuple-element.5) | copy-start | bytes 196612
